TPU v7x, 32 devices: a whole 2x2x4 slice. The times are simulated.
32 devices in a mesh: win: 4 (over y, x), row: 2 (over core), col: 4 (over z).
Axes of the slice: x: 2, y: 2, z: 4, core: 2. Of those that a mesh axis runs over, the one named last changes fastest.
Arguments:
- spectra: bfloat16 [2, 8, 6144, 768], P(None, None, ('row', 'col'), 'win'), may hold values from -6 to 6
- gain: float32 [6144], P(('row', 'col')), may hold values from 0.1 to 3
Outputs:
- cross: float32 [2, 8, 6144, 6144], P(None, 'win', 'row', 'col')
All inputs are finite; a program needn't handle non-finite values.
Results may differ from a plain program's by a relative error of at most 0.0038.
Values may be sent and summed in bfloat16 or wider, within the bound.
A program may use at most 256 MiB of HBM per device.

v0:
```python
import jax
import jax.numpy as jnp
from jax import lax
from jax.sharding import PartitionSpec as P


def broadcast(value, axis, source):
    kept = jnp.where(lax.axis_index(axis) == source, value, 0).astype(value.dtype)
    return lax.psum(kept, axis)


def per_device(spectra, gain):
    calibrated = spectra.astype(jnp.float32) * gain[None, None, :, None]
    level = jnp.sqrt(jnp.mean(calibrated * calibrated, axis=(0, 1)))
    white = (calibrated / jnp.maximum(level, 0.5)).astype(jnp.bfloat16)
    regrouped = lax.all_to_all(white, "win", split_axis=1, concat_axis=3, tiled=True)
    windows = regrouped.shape[3]
    rows_block = lax.all_gather(regrouped, "col", axis=2, tiled=True)
    ratio = lax.axis_size("col") // lax.axis_size("row")
    col_width = rows_block.shape[2] // ratio
    col_index = lax.axis_index("col")
    portion = col_index % ratio
    root_row = col_index // ratio
    relayed = broadcast(rows_block, "row", root_row)
    cols_block = lax.dynamic_slice_in_dim(relayed, portion * col_width, col_width, 2)
    left_side = jnp.concatenate([rows_block[0], rows_block[1]], axis=-1)
    right_real = jnp.concatenate([cols_block[0], cols_block[1]], axis=-1)
    right_imag = jnp.concatenate([-cols_block[1], cols_block[0]], axis=-1)
    right_both = jnp.stack([right_real, right_imag])
    stacked = jnp.einsum(
        "fiw,ofjw->ofij", left_side, right_both, preferred_element_type=jnp.float32
    )
    return stacked / jnp.float32(windows)


def solution(mesh):
    in_specs = (P(None, None, ("row", "col"), "win"), P(("row", "col")))
    out_specs = P(None, "win", "row", "col")
    return jax.shard_map(
        per_device, mesh=mesh, in_specs=in_specs, out_specs=out_specs, check_vma=False
    )
```

profile of v0, /device:TPU:0, one launch (start us, length us, event | category | flops | bytes accessed | tf_op | source)
XLA Modules:
  0.0 643.1 jit_solution(993827543162699644)
XLA Ops:
  6.5 0.0 all-gather.2.cloned.1.call-start
  6.5 0.0 copy-start
  6.5 3.8 multiply_reduce_fusion
  10.3 0.2 sqrt_maximum_fusion
  10.5 0.0 copy-done
  10.5 1.9 divide_convert_fusion
  12.5 58.4 %all_to_all.18 = bf16[2,8,768,192]{2,3,0,1:T(8,128)(2,1)S(1)} all-to-all(bf16[2,8,768,192]{2,3,0,1:T(8,128)(2,1)S(1)} %divide_convert_fusion), channel_id=1, replica_groups=mesh['win'=4,'row'=2,'col'=4] {'win'}, dimensions={1} | all-to-all | bytes 9437184 | tf_op jit(solution)/shard_map/all_to_all | solution.py:16
  70.9 2.6 copy.15
  73.5 6.7 %copy.16 = bf16[2,2,768,768]{3,2,1,0:T(8,128)(2,1)} copy(bf16[2,2,768,768]{2,3,1,0:T(8,128)(2,1)} %bitcast.30) | data formatting | bytes 9437184 | tf_op jit(solution)/shard_map/all_to_all | solution.py:16
  80.2 0.0 all-gather.2.cloned.1.call-update
  80.2 0.2 all-reduce.2.cloned.1.call-start
  80.5 321.8 %all-gather.2.cloned.1.call-done = bf16[2,2,3072,768]{3,2,1,0:T(8,128)(2,1)} async-done(((bf16[2,2,768,768]{3,2,1,0:T(8,128)(2,1)}), bf16[2,2,3072,768]{3,2,1,0:T(8,128)(2,1)}) %all-gather.2.cloned.1.call-update) | async-done | bytes 18874384 | tf_op jit(solution)/shard_map/all_gather | solution.py:18
  402.2 16.7 %broadcast_select_fusion = bf16[2,2,3072,768]{3,2,1,0:T(8,128)(2,1)} fusion(bf16[2,2,3072,768]{3,2,1,0:T(8,128)(2,1)} %all-gather.2.cloned.1.call-done, pred[]{:T(512)S(6)} %eq.5), kind=kLoop, calls=%fused_computation.6 | loop fusion | flops 9437184 | bytes 37748736 | tf_op jit(solution)/shard_map/jit(_where)/select_n | solution.py:8
  418.9 0.0 all-reduce.2.cloned.1.call-update
  418.9 16.4 %slice_bitcast_fusion.1 = (bf16[2,3072,768]{2,1,0:T(8,128)(2,1)}, bf16[2,3072,768]{2,1,0:T(8,128)(2,1)}) fusion(bf16[2,2,3072,768]{3,2,1,0:T(8,128)(2,1)} %all-gather.2.cloned.1.call-done), kind=kLoop, calls=%fused_computation.8 | loop fusion | bytes 37748736 | tf_op jit(solution)/shard_map/squeeze | solution.py:26
  435.3 45.7 %all-reduce.2.cloned.1.call-done = bf16[2,2,3072,768]{3,2,1,0:T(8,128)(2,1)} async-done(((bf16[2,2,3072,768]{3,2,1,0:T(8,128)(2,1)}), bf16[2,2,3072,768]{3,2,1,0:T(8,128)(2,1)}) %all-reduce.2.cloned.1.call-update) | async-done | bytes 18874384 | tf_op jit(solution)/shard_map/psum | solution.py:9
  481.0 2.6 dynamic-slice_bitcast_fusion.1
  483.6 3.6 fusion.4
  487.2 7.0 %maximum_bitcast_fusion.2 = (bf16[1,2,1536,1536]{3,2,1,0:T(8,128)(2,1)}, bf16[1,2,1536,1536]{3,2,1,0:T(8,128)(2,1)}) fusion(bf16[2,1536,768]{2,1,0:T(8,128)(2,1)S(1)} %get-tuple-element.6, bf16[2,1536,768]{2,1,0:T(8,128)(2,1)S(1)} %dynamic-slice_bitcast_fusion.1, bf16[2,1536,768]{2,1,0:T(8,128)(2,1)S(1)} %get-tuple-element.5), kind=kLoop, calls=%fused_computation.9 | loop fusion | flops 37748736 | bytes 33030144 | tf_op jit(solution)/shard_map/stack | solution.py:29
  494.2 69.0 %multiply_bitcast_fusion = f32[2,2,3072,1536]{2,3,0,1:T(8,128)} fusion(bf16[2,3072,768]{2,1,0:T(8,128)(2,1)} %get-tuple-element.8, bf16[2,3072,768]{2,1,0:T(8,128)(2,1)} %get-tuple-element.7, bf16[1,2,1536,1536]{3,2,1,0:T(8,128)(2,1)} %get-tuple-element.10, bf16[1,2,1536,1536]{3,2,1,0:T(8,128)(2,1)} %get-tuple-element.9), kind=kOutput, calls=%fused_computation | convolution fusion | flops 58048118784 | bytes 113246208 | tf_op jit(solution)/shard_map/fiw,ofjw->ofij/dot_general | solution.py:30
  563.2 73.1 %copy.18 = f32[2,2,3072,1536]{3,2,1,0:T(8,128)} copy(f32[2,2,3072,1536]{2,3,0,1:T(8,128)} %multiply_bitcast_fusion) | data formatting | bytes 150994944 | tf_op jit(solution)/shard_map/div | solution.py:33
Async XLA Ops:
  6.5 395.7 %all-gather.2.cloned.1.call-start = ((), (), s32[]{:S(2)}) async-start(), calls=%async_computation.1 | async-start | bytes 23592960 | tf_op jit(solution)/shard_map/all_gather | solution.py:18
  6.5 4.0 copy-start
  80.2 400.8 %all-reduce.2.cloned.1.call-start = ((), (), s32[]{:S(2)}) async-start(), calls=%async_computation.2 | async-start | bytes 37748736 | tf_op jit(solution)/shard_map/psum | solution.py:9
Sparse Core Ops, SparseCore 0:
  80.3 321.8 all-gather.1
  419.1 61.8 all-reduce.1
where the time goes:
time: 645 us; the launch traced here: 643 us
  waiting for transfers between devices  367 us (57%)
  local copies, waits for them, and re-layouts  101 us (16%)
  matrix products  69 us (11%)
  blocking collectives  58.4 us (9%)
  other arithmetic  33.1 us (5%)
  between operations  13.5 us (2%)
    all_gather x1, waiting for transfers between devices, per_device(): rows_block = lax.all_gather(regrouped, 'col', axis=2, tiled=True)  322 us
    div x1, local copies, waits for them, and re-layouts, per_device(): return stacked / jnp.float32(windows)  73.1 us
    dot_general x1, matrix products, per_device(): jnp.einsum('fiw,ofjw->ofij', left_side, right_both, preferred_element_typ...  69 us
    all_to_all x1, blocking collectives, per_device(): lax.all_to_all(white, 'win', split_axis=1, concat_axis=3, tiled=True)  58.4 us
    psum x1, waiting for transfers between devices, broadcast(): return lax.psum(kept, axis)  45.7 us
    select_n x1, other arithmetic, broadcast(): jnp.where(lax.axis_index(axis) == source, value, 0).astype(value.dtype)  16.7 us
    squeeze x1, local copies, waits for them, and re-layouts, per_device(): left_side = jnp.concatenate([rows_block[0], rows_block[1]], axis=-1)  16.4 us
  transfers between devices with their start and end apart: 2, of which 2 were waited for; matrix products, arithmetic and copies ran while one was open for 3% of the time, Pallas kernels for 0%

commit v1 on v0

--- a/solution.py
+++ b/solution.py
@@ -1,7 +1,13 @@
+import functools
+
 import jax
 import jax.numpy as jnp
 from jax import lax
+from jax.experimental import pallas as pl
+from jax.experimental.pallas import tpu as pltpu
 from jax.sharding import PartitionSpec as P
+
+MESH = pl.DeviceIdType.MESH
 
 
 def broadcast(value, axis, source):
@@ -9,7 +15,7 @@
     return lax.psum(kept, axis)
 
 
-def per_device(spectra, gain):
+def per_device_collectives(spectra, gain):
     calibrated = spectra.astype(jnp.float32) * gain[None, None, :, None]
     level = jnp.sqrt(jnp.mean(calibrated * calibrated, axis=(0, 1)))
     white = (calibrated / jnp.maximum(level, 0.5)).astype(jnp.bfloat16)
@@ -33,9 +39,306 @@
     return stacked / jnp.float32(windows)
 
 
+def whiten_kernel(x_ref, gain_ref, white_ref):
+    parts, bins = x_ref.shape[:2]
+    gain = gain_ref[...]
+    total = jnp.zeros(x_ref.shape[2:], jnp.float32)
+    for p in range(parts):
+        for f in range(bins):
+            calibrated = x_ref[p, f].astype(jnp.float32) * gain
+            total += calibrated * calibrated
+    level = jnp.sqrt(total * (1.0 / (parts * bins)))
+    scale = 1.0 / jnp.maximum(level, 0.5)
+    for p in range(parts):
+        for f in range(bins):
+            calibrated = x_ref[p, f].astype(jnp.float32) * gain
+            white_ref[f, p] = (calibrated * scale).astype(white_ref.dtype)
+
+
+def whiten(spectra, gain):
+    parts, bins, channels, windows = spectra.shape
+    tile = 32 if windows % 32 == 0 else 16
+    return pl.pallas_call(
+        whiten_kernel,
+        grid=(windows // tile,),
+        out_shape=jax.ShapeDtypeStruct((bins, parts, windows, channels), jnp.bfloat16),
+        in_specs=[
+            pl.BlockSpec((parts, bins, tile, channels), lambda i: (0, 0, i, 0)),
+            pl.BlockSpec((1, channels), lambda i: (0, 0)),
+        ],
+        out_specs=pl.BlockSpec((bins, parts, tile, channels), lambda i: (0, 0, i, 0)),
+        compiler_params=pltpu.CompilerParams(vmem_limit_bytes=32 * 2**20),
+    )(jnp.swapaxes(spectra, 2, 3), gain[None])
+
+
+class Gather:
+    def __init__(self, sizes, white, rows, cols, sems):
+        self.S, self.R, self.N = sizes
+        self.white, self.rows, self.cols = white, rows, cols
+        (self.own_sem, self.swap_send, self.swap_recv, self.down_send, self.down_recv, self.up_send, self.up_recv,
+         self.col_own, self.col_send, self.col_recv) = sems
+        self.w, self.r, self.c = lax.axis_index("win"), lax.axis_index("row"), lax.axis_index("col")
+        self.bins = rows.shape[0]
+        ratio = self.N // self.R
+        self.first_col = (self.c % ratio) * self.R
+        self.is_root = self.r == self.c // ratio
+        self.col_reach = max(
+            abs((c % ratio) * self.R + q - c) for c in range(self.N) for q in range(self.R)
+        )
+
+    def partner(self, d):
+        half = self.S // 2
+        return ((self.w // 2 + d // 2) % half) * 2 + (self.w + d) % 2
+
+    def barrier(self):
+        sem = pltpu.get_barrier_semaphore()
+        for d in range(1, self.S):
+            pl.semaphore_signal(sem, inc=1, device_id={"win": self.partner(d)}, device_id_type=MESH)
+        for e in range(1, self.R):
+            pl.semaphore_signal(sem, inc=1, device_id={"row": (self.r + e) % self.R}, device_id_type=MESH)
+
+        @pl.when(self.c > 0)
+        def _():
+            pl.semaphore_signal(sem, inc=1, device_id={"col": self.c - 1}, device_id_type=MESH)
+
+        @pl.when(self.c < self.N - 1)
+        def _():
+            pl.semaphore_signal(sem, inc=1, device_id={"col": self.c + 1}, device_id_type=MESH)
+
+        ends = (self.c == 0).astype(jnp.int32) + (self.c == self.N - 1).astype(jnp.int32)
+        pl.semaphore_wait(sem, self.S - 1 + self.R - 1 + 2 - ends)
+
+    def keep(self, b):
+        return pltpu.make_async_copy(self.white.at[self.w, b], self.rows.at[b, self.c, 0], self.own_sem.at[b])
+
+    def swap(self, b, d):
+        p = self.partner(d)
+        return pltpu.make_async_remote_copy(
+            src_ref=self.white.at[p, b], dst_ref=self.rows.at[b, self.c, d],
+            send_sem=self.swap_send.at[b, d], recv_sem=self.swap_recv.at[b, d],
+            device_id={"win": p}, device_id_type=MESH)
+
+    def down(self, b, t, d):
+        block = self.c + t
+        src = self.white.at[self.w, b] if t == 0 and d == 0 else self.rows.at[b, block, d]
+        return pltpu.make_async_remote_copy(
+            src_ref=src, dst_ref=self.rows.at[b, block, d],
+            send_sem=self.down_send.at[b, t, d], recv_sem=self.down_recv.at[b, t, d],
+            device_id={"col": self.c - 1}, device_id_type=MESH)
+
+    def up(self, b, t, d):
+        block = self.c - t
+        src = self.white.at[self.w, b] if t == 0 and d == 0 else self.rows.at[b, block, d]
+        return pltpu.make_async_remote_copy(
+            src_ref=src, dst_ref=self.rows.at[b, block, d],
+            send_sem=self.up_send.at[b, t, d], recv_sem=self.up_recv.at[b, t, d],
+            device_id={"col": self.c + 1}, device_id_type=MESH)
+
+    def landed(self, b, block, d, sem):
+        ref = self.rows.at[b, block, d]
+        pltpu.make_async_copy(ref, ref, sem).wait()
+
+    def col_keep(self, b, q):
+        return pltpu.make_async_copy(
+            self.rows.at[b, self.first_col + q], self.cols.at[b, q], self.col_own.at[b, q])
+
+    def col_pass(self, b, q, e):
+        return pltpu.make_async_remote_copy(
+            src_ref=self.rows.at[b, self.first_col + q], dst_ref=self.cols.at[b, q],
+            send_sem=self.col_send.at[b, q, e], recv_sem=self.col_recv.at[b, q],
+            device_id={"row": (self.r + e) % self.R}, device_id_type=MESH)
+
+    def start_swaps(self, b):
+        self.keep(b).start()
+        for d in range(1, self.S):
+            self.swap(b, d).start()
+
+    def down_goes(self, t):
+        return jnp.logical_and(self.c > 0, self.c + t < self.N)
+
+    def up_goes(self, t):
+        return jnp.logical_and(self.c < self.N - 1, self.c - t >= 0)
+
+    def send_own(self, b):
+        for d in range(self.S):
+            if d:
+                self.landed(b, self.c, d, self.swap_recv.at[b, d])
+            pl.when(self.down_goes(0))(lambda d=d: self.down(b, 0, d).start())
+            pl.when(self.up_goes(0))(lambda d=d: self.up(b, 0, d).start())
+
+    def forward_slot(self, b, t, d):
+        @pl.when(self.c + t < self.N)
+        def _():
+            self.landed(b, self.c + t, d, self.down_recv.at[b, t - 1, d])
+
+        if t < self.N - 1:
+            pl.when(self.down_goes(t))(lambda: self.down(b, t, d).start())
+
+        @pl.when(self.c - t >= 0)
+        def _():
+            self.landed(b, self.c - t, d, self.up_recv.at[b, t - 1, d])
+
+        if t < self.N - 1:
+            pl.when(self.up_goes(t))(lambda: self.up(b, t, d).start())
+
+        if t == self.col_reach and d == self.S - 1:
+            self.start_cols(b)
+
+    def start_cols(self, b):
+        self.keep(b).wait()
+
+        @pl.when(self.is_root)
+        def _():
+            for q in range(self.R):
+                for e in range(1, self.R):
+                    self.col_pass(b, q, e).start()
+                self.col_keep(b, q).start()
+
+    def wait_cols(self, b):
+        for q in range(self.R):
+            @pl.when(self.is_root)
+            def _():
+                self.col_keep(b, q).wait()
+
+            @pl.when(jnp.logical_not(self.is_root))
+            def _():
+                ref = self.cols.at[b, q]
+                pltpu.make_async_copy(ref, ref, self.col_recv.at[b, q]).wait()
+
+    def wait_sends(self):
+        for b in range(self.bins):
+            for d in range(1, self.S):
+                self.swap(b, d).wait_send()
+            for t in range(self.N - 1):
+                for d in range(self.S):
+                    pl.when(self.down_goes(t))(lambda: self.down(b, t, d).wait_send())
+                    pl.when(self.up_goes(t))(lambda: self.up(b, t, d).wait_send())
+
+            @pl.when(self.is_root)
+            def _():
+                for q in range(self.R):
+                    for e in range(1, self.R):
+                        self.col_pass(b, q, e).wait_send()
+
+
+def gather_kernel(sizes, white, rows, cols, *sems):
+    g = Gather(sizes, white, rows, cols, sems)
+    g.barrier()
+    g.start_swaps(0)
+    g.send_own(0)
+    for b in range(g.bins):
+        if b + 1 < g.bins:
+            g.start_swaps(b + 1)
+        for t in range(1, g.N):
+            for d in range(g.S):
+                g.forward_slot(b, t, d)
+            if t == 1 and b + 1 < g.bins:
+                g.send_own(b + 1)
+    for b in range(g.bins):
+        g.wait_cols(b)
+    g.wait_sends()
+
+
+def gather_semaphores(sizes, bins):
+    S, R, N = sizes
+    dma = pltpu.SemaphoreType.DMA
+    return [
+        dma((bins,)), dma((bins, S)), dma((bins, S)),
+        dma((bins, N, S)), dma((bins, N, S)), dma((bins, N, S)), dma((bins, N, S)),
+        dma((bins, R)), dma((bins, R, R)), dma((bins, R)),
+    ]
+
+
+def gather(white, sizes):
+    S, R, N = sizes
+    _, bins, parts, windows, channels = white.shape
+    slot = (parts, windows, channels)
+    return pl.pallas_call(
+        functools.partial(gather_kernel, sizes),
+        out_shape=(
+            jax.ShapeDtypeStruct((bins, N, S) + slot, white.dtype),
+            jax.ShapeDtypeStruct((bins, R, S) + slot, white.dtype),
+        ),
+        in_specs=[pl.BlockSpec(memory_space=pl.ANY)],
+        out_specs=(pl.BlockSpec(memory_space=pl.ANY), pl.BlockSpec(memory_space=pl.ANY)),
+        scratch_shapes=gather_semaphores(sizes, bins),
+        compiler_params=pltpu.CompilerParams(collective_id=0, has_side_effects=True),
+    )(white)
+
+
+def turn(right, S):
+    depth = right.shape[0] // (2 * S)
+    pieces = []
+    for s in range(S):
+        base = 2 * s * depth
+        pieces.append(-right[base + depth:base + 2 * depth])
+        pieces.append(right[base:base + depth])
+    return jnp.concatenate(pieces, axis=0)
+
+
+def stack_kernel(S, windows, left_ref, right_ref, out_ref, turned_ref):
+    blocks, _, width = right_ref.shape[1:]
+
+    @pl.when(pl.program_id(1) == 0)
+    def _():
+        for q in range(blocks):
+            turned_ref[q] = turn(right_ref[0, q], S)
+
+    left = left_ref[0, 0].T
+    for q in range(blocks):
+        where = slice(q * width, (q + 1) * width)
+        real = jnp.dot(left, right_ref[0, q], preferred_element_type=jnp.float32)
+        out_ref[0, 0, :, where] = real * (1.0 / windows)
+        imag = jnp.dot(left, turned_ref[q], preferred_element_type=jnp.float32)
+        out_ref[1, 0, :, where] = imag * (1.0 / windows)
+
+
+def stack(rows, cols, S):
+    bins, N, depth, channels = rows.shape
+    R = cols.shape[1]
+    tile = 384 if channels % 384 == 0 else 128
+    per = channels // tile
+    flops = 2 * 2 * bins * N * channels * R * channels * depth
+    return pl.pallas_call(
+        functools.partial(stack_kernel, S, depth // 2),
+        grid=(bins, N * per),
+        out_shape=jax.ShapeDtypeStruct((2, bins, N * channels, R * channels), jnp.float32),
+        in_specs=[
+            pl.BlockSpec((1, 1, depth, tile), lambda f, i: (f, i // per, 0, i % per)),
+            pl.BlockSpec((1, R, depth, channels), lambda f, i: (f, 0, 0, 0)),
+        ],
+        out_specs=pl.BlockSpec((2, 1, tile, R * channels), lambda f, i: (0, f, i, 0)),
+        scratch_shapes=[pltpu.VMEM((R, depth, channels), jnp.bfloat16)],
+        compiler_params=pltpu.CompilerParams(vmem_limit_bytes=56 * 2**20),
+        cost_estimate=pl.CostEstimate(flops=flops, bytes_accessed=10**8, transcendentals=0),
+    )(rows, cols)
+
+
+def per_device(sizes, spectra, gain):
+    S, R, N = sizes
+    parts, bins, channels, windows = spectra.shape
+    white = whiten(spectra, gain)
+    white = white.reshape(S, bins // S, parts, windows, channels)
+    rows, cols = gather(white, sizes)
+    depth = S * parts * windows
+    rows = rows.reshape(bins // S, N, depth, channels)
+    cols = cols.reshape(bins // S, R, depth, channels)
+    return stack(rows, cols, S)
+
+
 def solution(mesh):
+    sizes = mesh.shape["win"], mesh.shape["row"], mesh.shape["col"]
     in_specs = (P(None, None, ("row", "col"), "win"), P(("row", "col")))
     out_specs = P(None, "win", "row", "col")
+
+    def device_program(spectra, gain):
+        S, R, N = sizes
+        _, bins, channels, windows = spectra.shape
+        whole_tiles = channels % 128 == 0 and windows % 16 == 0
+        if whole_tiles and S % 2 == 0 and bins % S == 0 and N % R == 0 and R > 1:
+            return per_device(sizes, spectra, gain)
+        return per_device_collectives(spectra, gain)
+
     return jax.shard_map(
-        per_device, mesh=mesh, in_specs=in_specs, out_specs=out_specs, check_vma=False
+        device_program, mesh=mesh, in_specs=in_specs, out_specs=out_specs, check_vma=False
     )

time: 645 us -> 485 us (0.75)
  Pallas kernels: 0 us -> 480 us
  waiting for transfers between devices: 367 us -> 0 us
  local copies, waits for them, and re-layouts: 101 us -> 5.21 us
  matrix products: 69 us -> 0 us
  blocking collectives: 58.4 us -> 0 us
  other arithmetic: 33.1 us -> 0 us
  between operations: 13.5 us -> 0.03 us
    pallas_call x0 -> x3, Pallas kernels: none -> 480 us  [the longest x1 408 us: gather(): pl.pallas_call(functools.partial(gather_kernel, sizes), out_shape=(jax.Sh...]
    all_gather x1 -> x0, waiting for transfers between devices: 322 us -> none  [per_device(): rows_block = lax.all_gather(regrouped, 'col', axis=2, tiled=True)]
    div x1 -> x0, local copies, waits for them, and re-layouts: 73.1 us -> none  [per_device(): return stacked / jnp.float32(windows)]
    dot_general x1 -> x0, matrix products: 69 us -> none  [per_device(): jnp.einsum('fiw,ofjw->ofij', left_side, right_both, preferred_element_typ...]
    all_to_all x1 -> x0, blocking collectives: 58.4 us -> none  [per_device(): lax.all_to_all(white, 'win', split_axis=1, concat_axis=3, tiled=True)]
    psum x1 -> x0, waiting for transfers between devices: 45.7 us -> none  [broadcast(): return lax.psum(kept, axis)]
    squeeze x2 -> x0, local copies, waits for them, and re-layouts: 19 us -> none  [the longest x1 16.4 us: per_device(): left_side = jnp.concatenate([rows_block[0], rows_block[1]], axis=-1)]
    select_n x1 -> x0, other arithmetic: 16.7 us -> none  [broadcast(): jnp.where(lax.axis_index(axis) == source, value, 0).astype(value.dtype)]
  transfers between devices with their start and end apart: 2 -> 0, of which waited for: 2 -> 0; matrix products, arithmetic and copies ran while one was open for 3% -> 0% of each run, Pallas kernels for 0% -> 0%
where the time goes in v1:
time: 485 us
  Pallas kernels  480 us (99%)
  local copies, waits for them, and re-layouts  5.21 us (1%)
    pallas_call x1, Pallas kernels, gather(): pl.pallas_call(functools.partial(gather_kernel, sizes), out_shape=(jax.Sh...  408 us
    pallas_call x1, Pallas kernels, stack(): pl.pallas_call(functools.partial(stack_kernel, S, depth // 2), grid=(bins...  68.3 us

profile of v1, /device:TPU:0, one launch (start us, length us, event | category | flops | bytes accessed | tf_op | source)
XLA Modules:
  0.0 484.9 jit_solution(3218946618886023009)
XLA Ops:
  0.0 0.7 broadcast_in_dim.3.gain_ref
  0.7 0.0 copy-start.1
  0.7 2.3 copy-done.1
  3.0 3.1 shard_map.28
  6.2 0.0 copy-start
  6.2 2.2 copy-done
  8.3 408.2 %shard_map.29 = (bf16[2,4,4,2,192,768]{5,4,3,2,1,0:T(8,128)(2,1)}, bf16[2,2,4,2,192,768]{5,4,3,2,1,0:T(8,128)(2,1)}) custom-call(bf16[4,2,2,192,768]{4,3,2,1,0:T(8,128)(2,1)} %bitcast.4), custom_call_target="tpu_custom_call" | custom-call | tf_op jit(solution)/shard_map/pallas_call | solution.py:256
  416.6 68.3 %shard_map.30 = f32[2,2,3072,1536]{3,2,1,0:T(8,128)} custom-call(bf16[2,4,1536,768]{3,2,1,0:T(8,128)(2,1)} %bitcast.6, bf16[2,2,1536,768]{3,2,1,0:T(8,128)(2,1)} %bitcast.7), custom_call_target="tpu_custom_call" | custom-call | flops 57982058496 | bytes 100000000 | tf_op jit(solution)/shard_map/pallas_call | solution.py:302
Async XLA Ops:
  0.7 2.3 copy-start.1
  6.2 2.2 copy-start

commit v2 on v1

--- a/solution.py
+++ b/solution.py
@@ -76,7 +76,7 @@
         self.S, self.R, self.N = sizes
         self.white, self.rows, self.cols = white, rows, cols
         (self.own_sem, self.swap_send, self.swap_recv, self.down_send, self.down_recv, self.up_send, self.up_recv,
-         self.col_own, self.col_send, self.col_recv) = sems
+         self.col_send, self.col_recv, self.right_sem) = sems
         self.w, self.r, self.c = lax.axis_index("win"), lax.axis_index("row"), lax.axis_index("col")
         self.bins = rows.shape[0]
         ratio = self.N // self.R
@@ -138,10 +138,6 @@
         ref = self.rows.at[b, block, d]
         pltpu.make_async_copy(ref, ref, sem).wait()
 
-    def col_keep(self, b, q):
-        return pltpu.make_async_copy(
-            self.rows.at[b, self.first_col + q], self.cols.at[b, q], self.col_own.at[b, q])
-
     def col_pass(self, b, q, e):
         return pltpu.make_async_remote_copy(
             src_ref=self.rows.at[b, self.first_col + q], dst_ref=self.cols.at[b, q],
@@ -192,16 +188,11 @@
             for q in range(self.R):
                 for e in range(1, self.R):
                     self.col_pass(b, q, e).start()
-                self.col_keep(b, q).start()
 
     def wait_cols(self, b):
-        for q in range(self.R):
-            @pl.when(self.is_root)
-            def _():
-                self.col_keep(b, q).wait()
-
-            @pl.when(jnp.logical_not(self.is_root))
-            def _():
+        @pl.when(jnp.logical_not(self.is_root))
+        def _():
+            for q in range(self.R):
                 ref = self.cols.at[b, q]
                 pltpu.make_async_copy(ref, ref, self.col_recv.at[b, q]).wait()
 
@@ -221,7 +212,81 @@
                         self.col_pass(b, q, e).wait_send()
 
 
-def gather_kernel(sizes, white, rows, cols, *sems):
+def load_right(rows, cols, b, right, turned, sem):
+    R, S, depth, _ = right.shape
+    half = depth // 2
+    row, col = lax.axis_index("row"), lax.axis_index("col")
+    ratio = rows.shape[1] // R
+    first, is_root = (col % ratio) * R, row == col // ratio
+
+    @pl.when(is_root)
+    def _():
+        for q in range(R):
+            pltpu.make_async_copy(rows.at[b, first + q], right.at[q], sem.at[q]).start()
+
+    @pl.when(jnp.logical_not(is_root))
+    def _():
+        for q in range(R):
+            pltpu.make_async_copy(cols.at[b, q], right.at[q], sem.at[q]).start()
+
+    for q in range(R):
+        pltpu.make_async_copy(cols.at[b, q], right.at[q], sem.at[q]).wait()
+        for s in range(S):
+            turned[q, s, :half] = -right[q, s, half:]
+            turned[q, s, half:] = right[q, s, :half]
+
+
+def stack_tile(left, right, turned, put):
+    R, S, depth, width = right.shape
+    scale = 2.0 / (S * depth)
+    left = left.reshape(S * depth, left.shape[-1]).T
+    for q in range(R):
+        for part, side in enumerate((right, turned)):
+            block = side[q].reshape(S * depth, width)
+            total = jnp.dot(left, block, preferred_element_type=jnp.float32)
+            put(part, slice(q * width, (q + 1) * width), total * scale)
+
+
+def tile_of(channels):
+    return 384 if channels % 384 == 0 else 128
+
+
+def stack_early(g, b, early, left_buf, right, turned, out_buf, left_sem, out_sem):
+    load_right(g.rows, g.cols, b, right, turned, g.right_sem)
+    channels = right.shape[-1]
+    tile = left_buf.shape[-1]
+    per = channels // tile
+    count = g.N * per
+
+    def fetch(i):
+        lanes = pl.ds(pl.multiple_of((i % per) * tile, 128), tile)
+        return pltpu.make_async_copy(
+            g.rows.at[b, i // per, :, :, lanes], left_buf.at[i % 2], left_sem.at[i % 2])
+
+    def flush(i):
+        return pltpu.make_async_copy(
+            out_buf.at[i % 2], early.at[:, pl.ds(pl.multiple_of(i * tile, 128), tile), :], out_sem.at[i % 2])
+
+    fetch(0).start()
+
+    def step(i, carry):
+        pl.when(i + 1 < count)(lambda: fetch(i + 1).start())
+        fetch(i).wait()
+        pl.when(i >= 2)(lambda: flush(i - 2).wait())
+
+        def put(part, lanes, value):
+            out_buf[i % 2, part, :, lanes] = value
+
+        stack_tile(left_buf[i % 2], right, turned, put)
+        flush(i).start()
+        return carry
+
+    lax.fori_loop(0, count, step, 0)
+    flush(count - 2).wait()
+    flush(count - 1).wait()
+
+
+def gather_kernel(sizes, white, rows, cols, early, left_buf, right, turned, out_buf, left_sem, out_sem, *sems):
     g = Gather(sizes, white, rows, cols, sems)
     g.barrier()
     g.start_swaps(0)
@@ -234,8 +299,9 @@
                 g.forward_slot(b, t, d)
             if t == 1 and b + 1 < g.bins:
                 g.send_own(b + 1)
-    for b in range(g.bins):
         g.wait_cols(b)
+        if b == 0:
+            stack_early(g, b, early, left_buf, right, turned, out_buf, left_sem, out_sem)
     g.wait_sends()
 
 
@@ -245,85 +311,84 @@
     return [
         dma((bins,)), dma((bins, S)), dma((bins, S)),
         dma((bins, N, S)), dma((bins, N, S)), dma((bins, N, S)), dma((bins, N, S)),
-        dma((bins, R)), dma((bins, R, R)), dma((bins, R)),
+        dma((bins, R, R)), dma((bins, R)), dma((R,)),
     ]
 
 
 def gather(white, sizes):
     S, R, N = sizes
-    _, bins, parts, windows, channels = white.shape
-    slot = (parts, windows, channels)
+    _, bins, depth, channels = white.shape
+    tile = tile_of(channels)
+    flops = 2 * 2 * N * channels * R * channels * S * depth
     return pl.pallas_call(
         functools.partial(gather_kernel, sizes),
         out_shape=(
-            jax.ShapeDtypeStruct((bins, N, S) + slot, white.dtype),
-            jax.ShapeDtypeStruct((bins, R, S) + slot, white.dtype),
+            jax.ShapeDtypeStruct((bins, N, S, depth, channels), white.dtype),
+            jax.ShapeDtypeStruct((bins, R, S, depth, channels), white.dtype),
+            jax.ShapeDtypeStruct((2, N * channels, R * channels), jnp.float32),
         ),
         in_specs=[pl.BlockSpec(memory_space=pl.ANY)],
-        out_specs=(pl.BlockSpec(memory_space=pl.ANY), pl.BlockSpec(memory_space=pl.ANY)),
-        scratch_shapes=gather_semaphores(sizes, bins),
-        compiler_params=pltpu.CompilerParams(collective_id=0, has_side_effects=True),
+        out_specs=(pl.BlockSpec(memory_space=pl.ANY),) * 3,
+        scratch_shapes=[
+            pltpu.VMEM((2, S, depth, tile), white.dtype),
+            pltpu.VMEM((R, S, depth, channels), white.dtype),
+            pltpu.VMEM((R, S, depth, channels), white.dtype),
+            pltpu.VMEM((2, 2, tile, R * channels), jnp.float32),
+            pltpu.SemaphoreType.DMA((2,)),
+            pltpu.SemaphoreType.DMA((2,)),
+        ] + gather_semaphores(sizes, bins),
+        compiler_params=pltpu.CompilerParams(
+            collective_id=0, has_side_effects=True, vmem_limit_bytes=48 * 2**20),
+        cost_estimate=pl.CostEstimate(flops=flops, bytes_accessed=10**8, transcendentals=0),
     )(white)
 
 
-def turn(right, S):
-    depth = right.shape[0] // (2 * S)
-    pieces = []
-    for s in range(S):
-        base = 2 * s * depth
-        pieces.append(-right[base + depth:base + 2 * depth])
-        pieces.append(right[base:base + depth])
-    return jnp.concatenate(pieces, axis=0)
-
-
-def stack_kernel(S, windows, left_ref, right_ref, out_ref, turned_ref):
-    blocks, _, width = right_ref.shape[1:]
-
-    @pl.when(pl.program_id(1) == 0)
+def stack_kernel(left_ref, early_ref, rows, cols, out_ref, right, turned, sem):
+    @pl.when(pl.program_id(0) == 0)
     def _():
-        for q in range(blocks):
-            turned_ref[q] = turn(right_ref[0, q], S)
-
-    left = left_ref[0, 0].T
-    for q in range(blocks):
-        where = slice(q * width, (q + 1) * width)
-        real = jnp.dot(left, right_ref[0, q], preferred_element_type=jnp.float32)
-        out_ref[0, 0, :, where] = real * (1.0 / windows)
-        imag = jnp.dot(left, turned_ref[q], preferred_element_type=jnp.float32)
-        out_ref[1, 0, :, where] = imag * (1.0 / windows)
-
-
-def stack(rows, cols, S):
-    bins, N, depth, channels = rows.shape
+        load_right(rows, cols, 1, right, turned, sem)
+
+    out_ref[:, 0] = early_ref[...]
+
+    def put(part, lanes, value):
+        out_ref[part, 1, :, lanes] = value
+
+    stack_tile(left_ref[0, 0], right, turned, put)
+
+
+def stack(rows, cols, early):
+    bins, N, S, depth, channels = rows.shape
     R = cols.shape[1]
-    tile = 384 if channels % 384 == 0 else 128
+    tile = tile_of(channels)
     per = channels // tile
-    flops = 2 * 2 * bins * N * channels * R * channels * depth
+    flops = 2 * 2 * N * channels * R * channels * S * depth
     return pl.pallas_call(
-        functools.partial(stack_kernel, S, depth // 2),
-        grid=(bins, N * per),
+        stack_kernel,
+        grid=(N * per,),
         out_shape=jax.ShapeDtypeStruct((2, bins, N * channels, R * channels), jnp.float32),
         in_specs=[
-            pl.BlockSpec((1, 1, depth, tile), lambda f, i: (f, i // per, 0, i % per)),
-            pl.BlockSpec((1, R, depth, channels), lambda f, i: (f, 0, 0, 0)),
+            pl.BlockSpec((1, 1, S, depth, tile), lambda i: (1, i // per, 0, 0, i % per)),
+            pl.BlockSpec((2, tile, R * channels), lambda i: (0, i, 0)),
+            pl.BlockSpec(memory_space=pl.ANY),
+            pl.BlockSpec(memory_space=pl.ANY),
         ],
-        out_specs=pl.BlockSpec((2, 1, tile, R * channels), lambda f, i: (0, f, i, 0)),
-        scratch_shapes=[pltpu.VMEM((R, depth, channels), jnp.bfloat16)],
+        out_specs=pl.BlockSpec((2, bins, tile, R * channels), lambda i: (0, 0, i, 0)),
+        scratch_shapes=[
+            pltpu.VMEM((R, S, depth, channels), rows.dtype),
+            pltpu.VMEM((R, S, depth, channels), rows.dtype),
+            pltpu.SemaphoreType.DMA((R,)),
+        ],
         compiler_params=pltpu.CompilerParams(vmem_limit_bytes=56 * 2**20),
-        cost_estimate=pl.CostEstimate(flops=flops, bytes_accessed=10**8, transcendentals=0),
-    )(rows, cols)
+        cost_estimate=pl.CostEstimate(flops=flops, bytes_accessed=12 * 10**7, transcendentals=0),
+    )(rows, early, rows, cols)
 
 
 def per_device(sizes, spectra, gain):
     S, R, N = sizes
     parts, bins, channels, windows = spectra.shape
-    white = whiten(spectra, gain)
-    white = white.reshape(S, bins // S, parts, windows, channels)
-    rows, cols = gather(white, sizes)
-    depth = S * parts * windows
-    rows = rows.reshape(bins // S, N, depth, channels)
-    cols = cols.reshape(bins // S, R, depth, channels)
-    return stack(rows, cols, S)
+    white = whiten(spectra, gain).reshape(S, bins // S, parts * windows, channels)
+    rows, cols, early = gather(white, sizes)
+    return stack(rows, cols, early)
 
 
 def solution(mesh):
@@ -335,7 +400,7 @@
         S, R, N = sizes
         _, bins, channels, windows = spectra.shape
         whole_tiles = channels % 128 == 0 and windows % 16 == 0
-        if whole_tiles and S % 2 == 0 and bins % S == 0 and N % R == 0 and R > 1:
+        if whole_tiles and S % 2 == 0 and bins == 2 * S and N % R == 0 and R > 1:
             return per_device(sizes, spectra, gain)
         return per_device_collectives(spectra, gain)
 

time: 485 us -> 370 us (0.76)
  Pallas kernels: 480 us -> 366 us
    pallas_call x1, Pallas kernels: 408 us -> 312 us  [gather(): pl.pallas_call(functools.partial(gather_kernel, sizes), out_shape=(jax.Sh...]
    pallas_call x1, Pallas kernels: 68.3 us -> 51.6 us  [stack(): pl.pallas_call(stack_kernel, grid=(N * per,), out_shape=jax.ShapeDtypeStr...]
where the time goes in v2:
time: 370 us; the launch traced here: 369 us
  Pallas kernels  366 us (99%)
    pallas_call x1, Pallas kernels, gather(): pl.pallas_call(functools.partial(gather_kernel, sizes), out_shape=(jax.Sh...  312 us
    pallas_call x1, Pallas kernels, stack(): pl.pallas_call(stack_kernel, grid=(N * per,), out_shape=jax.ShapeDtypeStr...  51.6 us

profile of v2, /device:TPU:0, one launch (start us, length us, event | category | flops | bytes accessed | tf_op | source)
XLA Modules:
  0.0 369.5 jit_solution(590061456145758025)
XLA Ops:
  0.0 0.7 broadcast_in_dim.3.gain_ref
  0.7 0.0 copy-start
  0.7 2.3 copy-done
  3.0 3.1 shard_map.28
  6.2 311.7 %shard_map.29 = (bf16[2,4,4,384,768]{4,3,2,1,0:T(8,128)(2,1)}, bf16[2,2,4,384,768]{4,3,2,1,0:T(8,128)(2,1)}, f32[2,3072,1536]{2,1,0:T(8,128)}) custom-call(bf16[4,2,384,768]{3,2,1,0:T(8,128)(2,1)S(1)} %bitcast.3), custom_call_target="tpu_custom_call" | custom-call | flops 28991029248 | bytes 100000000 | tf_op jit(solution)/shard_map/pallas_call | solution.py:323
  317.9 51.6 %shard_map.30 = f32[2,2,3072,1536]{3,2,1,0:T(8,128)} custom-call(bf16[2,4,4,384,768]{4,3,2,1,0:T(8,128)(2,1)} %get-tuple-element.8.left_ref.rows, f32[2,3072,1536]{2,1,0:T(8,128)} %get-tuple-element.9.early_ref, bf16[2,4,4,384,768]{4,3,2,1,0:T(8,128)(2,1)} %get-tuple-element.8.left_ref.rows, bf16[2,2,4,384,768]{4,3,2,1,0:T(8,128)(2,1)} %get-tuple-element.10.cols), custom_call_target="tpu_custom_call" | custom-call | flops 28991029248 | bytes 120000000 | tf_op jit(solution)/shard_map/pallas_call | solution.py:365
Async XLA Ops:
  0.7 2.3 copy-start

commit v3 on v2

--- a/solution.py
+++ b/solution.py
@@ -212,7 +212,7 @@
                         self.col_pass(b, q, e).wait_send()
 
 
-def load_right(rows, cols, b, right, turned, sem):
+def load_right(rows, cols, b, right, turned, sem, meanwhile=None):
     R, S, depth, _ = right.shape
     half = depth // 2
     row, col = lax.axis_index("row"), lax.axis_index("col")
@@ -229,6 +229,8 @@
         for q in range(R):
             pltpu.make_async_copy(cols.at[b, q], right.at[q], sem.at[q]).start()
 
+    if meanwhile is not None:
+        meanwhile()
     for q in range(R):
         pltpu.make_async_copy(cols.at[b, q], right.at[q], sem.at[q]).wait()
         for s in range(S):
@@ -275,7 +277,7 @@
         pl.when(i >= 2)(lambda: flush(i - 2).wait())
 
         def put(part, lanes, value):
-            out_buf[i % 2, part, :, lanes] = value
+            out_buf[i % 2, part, :, lanes] = value.astype(out_buf.dtype)
 
         stack_tile(left_buf[i % 2], right, turned, put)
         flush(i).start()
@@ -325,7 +327,7 @@
         out_shape=(
             jax.ShapeDtypeStruct((bins, N, S, depth, channels), white.dtype),
             jax.ShapeDtypeStruct((bins, R, S, depth, channels), white.dtype),
-            jax.ShapeDtypeStruct((2, N * channels, R * channels), jnp.float32),
+            jax.ShapeDtypeStruct((2, N * channels, R * channels), white.dtype),
         ),
         in_specs=[pl.BlockSpec(memory_space=pl.ANY)],
         out_specs=(pl.BlockSpec(memory_space=pl.ANY),) * 3,
@@ -333,7 +335,7 @@
             pltpu.VMEM((2, S, depth, tile), white.dtype),
             pltpu.VMEM((R, S, depth, channels), white.dtype),
             pltpu.VMEM((R, S, depth, channels), white.dtype),
-            pltpu.VMEM((2, 2, tile, R * channels), jnp.float32),
+            pltpu.VMEM((2, 2, tile, R * channels), white.dtype),
             pltpu.SemaphoreType.DMA((2,)),
             pltpu.SemaphoreType.DMA((2,)),
         ] + gather_semaphores(sizes, bins),
@@ -344,11 +346,12 @@
 
 
 def stack_kernel(left_ref, early_ref, rows, cols, out_ref, right, turned, sem):
-    @pl.when(pl.program_id(0) == 0)
-    def _():
-        load_right(rows, cols, 1, right, turned, sem)
-
-    out_ref[:, 0] = early_ref[...]
+    def place():
+        out_ref[:, 0] = early_ref[...].astype(jnp.float32)
+
+    first = pl.program_id(0) == 0
+    pl.when(first)(lambda: load_right(rows, cols, 1, right, turned, sem, place))
+    pl.when(jnp.logical_not(first))(place)
 
     def put(part, lanes, value):
         out_ref[part, 1, :, lanes] = value

time: 370 us -> 362 us (0.978)
  Pallas kernels: 366 us -> 358 us
    pallas_call x1, Pallas kernels: 51.6 us -> 43.5 us  [stack(): pl.pallas_call(stack_kernel, grid=(N * per,), out_shape=jax.ShapeDtypeStr...]
where the time goes in v3:
time: 362 us; the launch traced here: 361 us
  Pallas kernels  358 us (99%)
    pallas_call x1, Pallas kernels, gather(): pl.pallas_call(functools.partial(gather_kernel, sizes), out_shape=(jax.Sh...  312 us
    pallas_call x1, Pallas kernels, stack(): pl.pallas_call(stack_kernel, grid=(N * per,), out_shape=jax.ShapeDtypeStr...  43.5 us

profile of v3, /device:TPU:0, one launch (start us, length us, event | category | flops | bytes accessed | tf_op | source)
XLA Modules:
  0.0 361.3 jit_solution(1075082341864417686)
XLA Ops:
  0.0 0.7 broadcast_in_dim.3.gain_ref
  0.7 0.0 copy-start
  0.7 2.3 copy-done
  3.0 3.1 shard_map.28
  6.2 311.7 %shard_map.29 = (bf16[2,4,4,384,768]{4,3,2,1,0:T(8,128)(2,1)}, bf16[2,2,4,384,768]{4,3,2,1,0:T(8,128)(2,1)}, bf16[2,3072,1536]{2,1,0:T(8,128)(2,1)}) custom-call(bf16[4,2,384,768]{3,2,1,0:T(8,128)(2,1)S(1)} %bitcast.3), custom_call_target="tpu_custom_call" | custom-call | flops 28991029248 | bytes 100000000 | tf_op jit(solution)/shard_map/pallas_call | solution.py:325
  317.9 43.5 %shard_map.30 = f32[2,2,3072,1536]{3,2,1,0:T(8,128)} custom-call(bf16[2,4,4,384,768]{4,3,2,1,0:T(8,128)(2,1)} %get-tuple-element.8.left_ref.rows, bf16[2,3072,1536]{2,1,0:T(8,128)(2,1)} %get-tuple-element.9.early_ref, bf16[2,4,4,384,768]{4,3,2,1,0:T(8,128)(2,1)} %get-tuple-element.8.left_ref.rows, bf16[2,2,4,384,768]{4,3,2,1,0:T(8,128)(2,1)} %get-tuple-element.10.cols), custom_call_target="tpu_custom_call" | custom-call | flops 28991029248 | bytes 120000000 | tf_op jit(solution)/shard_map/pallas_call | solution.py:368
Async XLA Ops:
  0.7 2.3 copy-start
